TPU v7x, 256 devices: a whole 4x4x8 slice. The times are simulated.
256 devices in a mesh: dp: 16 (over z, core), comp: 16 (over y, x).
Axes of the slice: x: 4, y: 4, z: 8, core: 2. Of those that a mesh axis runs over, the one named last changes fastest.
Arguments:
- points: bfloat16 [524288, 768], P(('dp', 'comp')), may hold values from -6 to 6
- candidates: int32 [4096, 4], P(('dp', 'comp')), may hold values from 0 to 511, as said below
- means: bfloat16 [65536, 768], P(('dp', 'comp')), may hold values from -0.59765625 to 0.59765625
- inv_var: bfloat16 [65536, 768], P(('dp', 'comp')), may hold values from 0.5 to 1.5
- log_weight: bfloat16 [65536], P(('dp', 'comp')), may hold values from -12 to -9
Outputs:
- counts: float32 [65536], P(('dp', 'comp'))
- first_moment: float32 [65536, 768], P(('dp', 'comp'))
- second_moment: float32 [65536, 768], P(('dp', 'comp'))
- loglik: float32 [524288], P(('dp', 'comp'))
Inputs may be any that keep to these rules, and one draw needn't show every extreme that they name: `candidates`: each row block names 4 different component blocks; all blocks b named by the row blocks of device index i along dp+comp satisfy (b // 2) % 16 == i % 16, that is, one owner group serves each device's rows.
All inputs are finite; a program needn't handle non-finite values.
Results may differ from a plain program's by a relative error of at most 0.028.
Values may be sent and summed in bfloat16 or wider, within the bound.
A program may use at most 128 MiB of HBM per device.

v0:
```python
import math
import jax
import jax.numpy as jnp
from jax import lax
from jax.sharding import PartitionSpec as P

CB = 128
RB = 128
CANDS = 4


def component_consts(mean_values, inv_values, log_values):
    feature_count = mean_values.shape[1]
    mean_f = mean_values.astype(jnp.float32)
    inv_f = inv_values.astype(jnp.float32)
    return (
        log_values.astype(jnp.float32)
        + 0.5 * jnp.sum(jnp.log(inv_f), axis=1)
        - 0.5 * jnp.sum(inv_f * mean_f * mean_f, axis=1)
        - 0.5 * feature_count * math.log(2.0 * math.pi)
    )


def block_terms(row_block, selector, scaled_flat, inverse_flat, constants):
    group_rows, slot_count, block_total = selector.shape
    feature_count = row_block.shape[2]
    row_f = row_block.astype(jnp.float32)
    squares = (row_f * row_f).astype(jnp.bfloat16)
    pick = selector.reshape(group_rows * slot_count, block_total)
    pick_bf = pick.astype(jnp.bfloat16)
    chosen_scaled = jnp.dot(pick_bf, scaled_flat, preferred_element_type=jnp.float32).astype(
        jnp.bfloat16
    )
    chosen_inverse = jnp.dot(pick_bf, inverse_flat, preferred_element_type=jnp.float32).astype(
        jnp.bfloat16
    )
    chosen_scaled = chosen_scaled.reshape(group_rows, slot_count, CB, feature_count)
    chosen_inverse = chosen_inverse.reshape(group_rows, slot_count, CB, feature_count)
    chosen_consts = jnp.dot(pick, constants, precision=lax.Precision.HIGHEST).reshape(
        group_rows, slot_count, CB
    )
    linear = jnp.einsum(
        "grd,gskd->grsk", row_block, chosen_scaled, preferred_element_type=jnp.float32
    )
    quadratic = jnp.einsum(
        "grd,gskd->grsk", squares, chosen_inverse, preferred_element_type=jnp.float32
    )
    densities = chosen_consts[:, None] + linear - 0.5 * quadratic
    row_peak = jnp.max(densities, axis=(2, 3))
    normalizer = row_peak + jnp.log(
        jnp.sum(jnp.exp(densities - row_peak[:, :, None, None]), axis=(2, 3))
    )
    responsibility = jnp.exp(densities - normalizer[:, :, None, None]).astype(jnp.bfloat16)
    counts = jnp.sum(responsibility.astype(jnp.float32), axis=1)
    first_moment = jnp.einsum(
        "grsk,grd->gskd", responsibility, row_block, preferred_element_type=jnp.float32
    )
    second_moment = jnp.einsum(
        "grsk,grd->gskd", responsibility, squares, preferred_element_type=jnp.float32
    )
    return (normalizer, counts, first_moment, second_moment)


def on_device(points, candidates, means, inv_var, log_weight):
    feature_count = points.shape[1]
    owner_count = lax.axis_size("comp")
    held_blocks = means.shape[0] // CB
    all_means, all_inverse, all_logs = (
        lax.all_gather(means, "dp", axis=0, tiled=True),
        lax.all_gather(inv_var, "dp", axis=0, tiled=True),
        lax.all_gather(log_weight, "dp", axis=0, tiled=True),
    )
    all_scaled = (all_inverse.astype(jnp.float32) * all_means.astype(jnp.float32)).astype(
        jnp.bfloat16
    )
    all_consts = component_consts(all_means, all_inverse, all_logs)
    group_blocks = all_scaled.shape[0] // CB
    scaled_flat = all_scaled.reshape(group_blocks, CB * feature_count)
    inverse_flat = all_inverse.reshape(group_blocks, CB * feature_count)
    constants = all_consts.reshape(group_blocks, CB)
    local_ids = candidates // (owner_count * held_blocks) * held_blocks + candidates % held_blocks
    block_count = candidates.shape[0]
    row_groups = points.reshape(block_count // 4, 4, RB, feature_count)
    id_groups = local_ids.reshape(block_count // 4, 4, CANDS)
    block_iota = jnp.arange(group_blocks, dtype=jnp.int32)

    def accumulate(running, inputs):
        row_block, chosen_ids = inputs
        selector = (chosen_ids[:, :, None] == block_iota[None, None, :]).astype(jnp.float32)
        normalizer, counts, first_part, second_part = block_terms(
            row_block, selector, scaled_flat, inverse_flat, constants
        )
        spread = selector.reshape(-1, group_blocks).T
        slot_total = spread.shape[1]
        new_counts = jnp.dot(
            spread, counts.reshape(slot_total, CB), precision=lax.Precision.HIGHEST
        )
        new_first = jnp.dot(
            spread,
            first_part.reshape(slot_total, CB * feature_count),
            precision=lax.Precision.HIGHEST,
        )
        new_second = jnp.dot(
            spread,
            second_part.reshape(slot_total, CB * feature_count),
            precision=lax.Precision.HIGHEST,
        )
        running = (running[0] + new_counts, running[1] + new_first, running[2] + new_second)
        return (running, normalizer)

    initial = (
        jnp.zeros((group_blocks, CB), jnp.float32),
        jnp.zeros((group_blocks, CB * feature_count), jnp.float32),
        jnp.zeros((group_blocks, CB * feature_count), jnp.float32),
    )
    partials, normalizers = lax.scan(accumulate, initial, (row_groups, id_groups))
    count_sum, first_sum, second_sum = (
        lax.psum_scatter(
            partials[0].astype(jnp.bfloat16), "dp", scatter_dimension=0, tiled=True
        ).astype(jnp.float32),
        lax.psum_scatter(
            partials[1].astype(jnp.bfloat16), "dp", scatter_dimension=0, tiled=True
        ).astype(jnp.float32),
        lax.psum_scatter(
            partials[2].astype(jnp.bfloat16), "dp", scatter_dimension=0, tiled=True
        ).astype(jnp.float32),
    )
    loglik = normalizers.reshape(-1) / feature_count
    return (
        count_sum.reshape(-1),
        first_sum.reshape(-1, feature_count),
        second_sum.reshape(-1, feature_count),
        loglik,
    )


def solution(mesh):
    return jax.shard_map(
        on_device,
        mesh=mesh,
        in_specs=(
            P(("dp", "comp"), None),
            P(("dp", "comp"), None),
            P(("dp", "comp"), None),
            P(("dp", "comp"), None),
            P(("dp", "comp")),
        ),
        out_specs=(
            P(("dp", "comp")),
            P(("dp", "comp"), None),
            P(("dp", "comp"), None),
            P(("dp", "comp")),
        ),
        check_vma=False,
    )
```

profile of v0, /device:TPU:2, one launch (start us, length us, event | category | flops | bytes accessed | tf_op | source)
XLA Modules:
  0.0 519.8 jit_solution(4086402239218131101)
XLA Ops:
  9.4 20.0 %all-gather = bf16[16,1,256]{2,1,0:T(2,128)(2,1)S(1)} all-gather(bf16[1,1,256]{2,1,0:T(2,128)(2,1)S(1)} %reshape.127), channel_id=1, replica_groups=mesh['dp'=16,'comp'=16] {'dp'}, dimensions={0}, use_global_device_ids=true | all-gather | bytes 8704 | tf_op jit(solution)/shard_map/all_gather | solution.py:71
  30.2 28.7 %all-gather.4.cloned.1.call-done = bf16[4096,768]{1,0:T(8,128)(2,1)} async-done(((bf16[256,768]{1,0:T(8,128)(2,1)}), bf16[4096,768]{1,0:T(8,128)(2,1)}) %all-gather.4.cloned.1.call-update) | async-done | bytes 6291472 | tf_op jit(solution)/shard_map/all_gather | solution.py:70
  58.9 46.5 %all-gather.6.cloned.1.call-done = bf16[4096,768]{1,0:T(8,128)(2,1)} async-done(((bf16[256,768]{1,0:T(8,128)(2,1)}), bf16[4096,768]{1,0:T(8,128)(2,1)}) %all-gather.6.cloned.1.call-update) | async-done | bytes 6291472 | tf_op jit(solution)/shard_map/all_gather | solution.py:69
  105.4 10.6 %fusion.32 = (f32[4096]{0:T(1024)S(1)}, f32[4096]{0:T(1024)S(1)}, bf16[4096,768]{1,0:T(8,128)(2,1)}) fusion(bf16[4096,768]{1,0:T(8,128)(2,1)} %all-gather.4.cloned.1.call-done, bf16[4096,768]{1,0:T(8,128)(2,1)} %all-gather.6.cloned.1.call-done), kind=kLoop, calls=%fused_computation.46 | loop fusion | flops 22011904 | bytes 18907136 | tf_op jit(solution)/shard_map/reduce_sum | solution.py:18
  115.9 7.2 %reshape.109 = bf16[32,98304]{1,0:T(8,128)(2,1)} reshape(bf16[4096,768]{1,0:T(8,128)(2,1)} %get-tuple-element.182) | data formatting | bytes 12582912 | tf_op jit(solution)/shard_map/reshape | solution.py:78
  123.2 7.3 %reshape.110 = bf16[32,98304]{1,0:T(8,128)(2,1)} reshape(bf16[4096,768]{1,0:T(8,128)(2,1)} %all-gather.4.cloned.1.call-done) | data formatting | bytes 12582912 | tf_op jit(solution)/shard_map/reshape | solution.py:79
  130.5 203.8 %while.18 = (s32[]{:T(128)}, f32[32,128]{1,0:T(8,128)S(1)}, f32[32,98304]{1,0:T(8,128)}, f32[32,98304]{1,0:T(8,128)}, f32[4,4,128]{2,1,0:T(4,128)S(1)}, /*index=...) while((s32[]{:T(128)}, f32[32,128]{1,0:T(8,128)S(1)}, ...), condition=%wide.region_6.7_spmd.clone.clone, body=%wide.region_2.6_spmd.clone.clone.sunk | while | flops 3042191872 | bytes 255429680 | solution.py:116
  144.2 6.3 %copy.24 = f32[2,8,128,768]{3,1,2,0:T(8,128)} copy(f32[2,8,128,768]{3,2,1,0:T(8,128)S(1)} %bitcast.122) | data formatting | bytes 12582912 | tf_op jit(solution)/shard_map/while
  150.5 10.6 %convolution_add_fusion.7 = f32[32,98304]{1,0:T(8,128)} fusion(f32[16,98304]{1,0:T(8,128)} %bitcast.119, f32[32,98304]{1,0:T(8,128)} %get-tuple-element.272, pred[]{:T(512)S(6)} %compare.6, s32[16]{0:T(128)S(1)} %eq.108), kind=kOutput, calls=%fused_computation.2.clone.1 | convolution fusion | flops 610271744 | bytes 31457344 | tf_op jit(solution)/shard_map/while/body/eval_jaxpr/dot_general | solution.py:98
  167.0 8.2 %convolution_add_fusion.8 = f32[32,98304]{1,0:T(8,128)S(1)} fusion(f32[16,98304]{1,0:T(8,128)S(1)} %bitcast.120, f32[32,98304]{1,0:T(8,128)S(1)} %bitcast.126, pred[]{:T(512)S(6)} %compare.6, s32[16]{0:T(128)S(1)} %eq.108), kind=kOutput, calls=%fused_computation.1.clone.1 | convolution fusion | flops 610271744 | bytes 31457344 | tf_op jit(solution)/shard_map/while/body/eval_jaxpr/dot_general | solution.py:103
  175.3 4.5 copy-done
  193.7 6.3 %copy.24 = f32[2,8,128,768]{3,1,2,0:T(8,128)} copy(f32[2,8,128,768]{3,2,1,0:T(8,128)S(1)} %bitcast.122) | data formatting | bytes 12582912 | tf_op jit(solution)/shard_map/while
  200.0 12.5 %convolution_add_fusion.7 = f32[32,98304]{1,0:T(8,128)} fusion(f32[16,98304]{1,0:T(8,128)} %bitcast.119, f32[32,98304]{1,0:T(8,128)} %get-tuple-element.272, pred[]{:T(512)S(6)} %compare.6, s32[16]{0:T(128)S(1)} %eq.108), kind=kOutput, calls=%fused_computation.2.clone.1 | convolution fusion | flops 610271744 | bytes 31457344 | tf_op jit(solution)/shard_map/while/body/eval_jaxpr/dot_general | solution.py:98
  218.4 8.2 %convolution_add_fusion.8 = f32[32,98304]{1,0:T(8,128)S(1)} fusion(f32[16,98304]{1,0:T(8,128)S(1)} %bitcast.120, f32[32,98304]{1,0:T(8,128)S(1)} %bitcast.126, pred[]{:T(512)S(6)} %compare.6, s32[16]{0:T(128)S(1)} %eq.108), kind=kOutput, calls=%fused_computation.1.clone.1 | convolution fusion | flops 610271744 | bytes 31457344 | tf_op jit(solution)/shard_map/while/body/eval_jaxpr/dot_general | solution.py:103
  245.0 6.3 %copy.24 = f32[2,8,128,768]{3,1,2,0:T(8,128)} copy(f32[2,8,128,768]{3,2,1,0:T(8,128)S(1)} %bitcast.122) | data formatting | bytes 12582912 | tf_op jit(solution)/shard_map/while
  251.3 12.5 %convolution_add_fusion.7 = f32[32,98304]{1,0:T(8,128)} fusion(f32[16,98304]{1,0:T(8,128)} %bitcast.119, f32[32,98304]{1,0:T(8,128)} %get-tuple-element.272, pred[]{:T(512)S(6)} %compare.6, s32[16]{0:T(128)S(1)} %eq.108), kind=kOutput, calls=%fused_computation.2.clone.1 | convolution fusion | flops 610271744 | bytes 31457344 | tf_op jit(solution)/shard_map/while/body/eval_jaxpr/dot_general | solution.py:98
  269.8 8.2 %convolution_add_fusion.8 = f32[32,98304]{1,0:T(8,128)S(1)} fusion(f32[16,98304]{1,0:T(8,128)S(1)} %bitcast.120, f32[32,98304]{1,0:T(8,128)S(1)} %bitcast.126, pred[]{:T(512)S(6)} %compare.6, s32[16]{0:T(128)S(1)} %eq.108), kind=kOutput, calls=%fused_computation.1.clone.1 | convolution fusion | flops 610271744 | bytes 31457344 | tf_op jit(solution)/shard_map/while/body/eval_jaxpr/dot_general | solution.py:103
  296.4 6.3 %copy.24 = f32[2,8,128,768]{3,1,2,0:T(8,128)} copy(f32[2,8,128,768]{3,2,1,0:T(8,128)S(1)} %bitcast.122) | data formatting | bytes 12582912 | tf_op jit(solution)/shard_map/while
  302.7 12.5 %convolution_add_fusion.7 = f32[32,98304]{1,0:T(8,128)} fusion(f32[16,98304]{1,0:T(8,128)} %bitcast.119, f32[32,98304]{1,0:T(8,128)} %get-tuple-element.272, pred[]{:T(512)S(6)} %compare.6, s32[16]{0:T(128)S(1)} %eq.108), kind=kOutput, calls=%fused_computation.2.clone.1 | convolution fusion | flops 610271744 | bytes 31457344 | tf_op jit(solution)/shard_map/while/body/eval_jaxpr/dot_general | solution.py:98
  321.1 8.2 %convolution_add_fusion.8 = f32[32,98304]{1,0:T(8,128)S(1)} fusion(f32[16,98304]{1,0:T(8,128)S(1)} %bitcast.120, f32[32,98304]{1,0:T(8,128)S(1)} %bitcast.126, pred[]{:T(512)S(6)} %compare.6, s32[16]{0:T(128)S(1)} %eq.108), kind=kOutput, calls=%fused_computation.1.clone.1 | convolution fusion | flops 610271744 | bytes 31457344 | tf_op jit(solution)/shard_map/while/body/eval_jaxpr/dot_general | solution.py:103
  334.3 7.9 %convert_element_type.56 = bf16[32,98304]{1,0:T(8,128)(2,1)} convert(f32[32,98304]{1,0:T(8,128)} %get-tuple-element.68) | non-fusion elementwise | flops 3145728 | bytes 18874368 | tf_op jit(solution)/shard_map/convert_element_type | solution.py:122
  342.2 7.9 %convert_element_type.57 = bf16[32,98304]{1,0:T(8,128)(2,1)} convert(f32[32,98304]{1,0:T(8,128)} %get-tuple-element.69) | non-fusion elementwise | flops 3145728 | bytes 18874368 | tf_op jit(solution)/shard_map/convert_element_type | solution.py:125
  352.0 26.5 %all-reduce = bf16[32,128]{1,0:T(8,128)(2,1)S(1)} all-reduce(bf16[32,128]{1,0:T(8,128)(2,1)S(1)} %convert_element_type.55), channel_id=2, replica_groups=mesh['dp'=16,'comp'=16] {'dp'}, use_global_device_ids=true, to_apply=%region_7.8.clone | all-reduce | flops 4096 | bytes 16384
  379.6 128.0 %all-reduce.6.cloned.1.call-done = (bf16[32,98304]{1,0:T(8,128)(2,1)}, bf16[32,98304]{1,0:T(8,128)(2,1)}) async-done(((bf16[32,98304]{1,0:T(8,128)(2,1)}, bf16[32,98304]{1,0:T(8,128)(2,1)}), (bf16[32,98304]{1,0:T(8,128)(2,1)}, bf16[32,98304]{1,0:T(8,128)(2,1)})) %all-reduce.6.cloned.1.call-update) | async-done | bytes 12582928
  (147 shorter events, 103.4 us)
Async XLA Ops:
  7.2 51.7 %all-gather.4.cloned.1.call-start = ((), (), s32[]{:S(2)}) async-start(), calls=%async_computation | async-start | bytes 6684672 | tf_op jit(solution)/shard_map/all_gather | solution.py:70
  7.9 97.5 %all-gather.6.cloned.1.call-start = ((), (), s32[]{:S(2)}) async-start(), calls=%async_computation.1 | async-start | bytes 6684672 | tf_op jit(solution)/shard_map/all_gather | solution.py:69
  8.6 499.0 %all-reduce.6.cloned.1.call-start = ((), (), s32[]{:S(2)}) async-start(), calls=%async_computation.2 | async-start | bytes 25165824
  130.6 7.0 %slice-start.3 = ((s8[6291456]{0:T(1024)(128)(4,1)}), s8[4194304]{0:T(1024)(128)(4,1)S(1)}, s32[]{:S(2)}) async-start(s8[6291456]{0:T(1024)(128)(4,1)} %bitcast.129), calls=%async_computation.6 | async-start | bytes 8388608 | tf_op jit(solution)/shard_map/while
  150.5 16.6 %slice-start = ((s8[12582912]{0:T(1024)(128)(4,1)}), s8[4194304]{0:T(1024)(128)(4,1)S(1)}, s32[]{:S(2)}) async-start(s8[12582912]{0:T(1024)(128)(4,1)} %bitcast.125), calls=%async_computation.3 | async-start | bytes 8388608 | tf_op jit(solution)/shard_map/while
  150.5 16.6 %slice-start.1 = ((s8[12582912]{0:T(1024)(128)(4,1)}), s8[4194304]{0:T(1024)(128)(4,1)S(1)}, s32[]{:S(2)}) async-start(s8[12582912]{0:T(1024)(128)(4,1)} %bitcast.125), calls=%async_computation.4 | async-start | bytes 8388608 | tf_op jit(solution)/shard_map/while
  161.1 5.9 %slice-start.2 = ((s8[12582912]{0:T(1024)(128)(4,1)}), s8[4194304]{0:T(1024)(128)(4,1)S(1)}, s32[]{:S(2)}) async-start(s8[12582912]{0:T(1024)(128)(4,1)} %bitcast.125), calls=%async_computation.5 | async-start | bytes 8388608 | tf_op jit(solution)/shard_map/while
  175.2 4.5 copy-start
  180.1 7.0 %slice-start.3 = ((s8[6291456]{0:T(1024)(128)(4,1)}), s8[4194304]{0:T(1024)(128)(4,1)S(1)}, s32[]{:S(2)}) async-start(s8[6291456]{0:T(1024)(128)(4,1)} %bitcast.129), calls=%async_computation.6 | async-start | bytes 8388608 | tf_op jit(solution)/shard_map/while
  184.1 3.1 slice-start.4
  200.0 18.4 %slice-start = ((s8[12582912]{0:T(1024)(128)(4,1)}), s8[4194304]{0:T(1024)(128)(4,1)S(1)}, s32[]{:S(2)}) async-start(s8[12582912]{0:T(1024)(128)(4,1)} %bitcast.125), calls=%async_computation.3 | async-start | bytes 8388608 | tf_op jit(solution)/shard_map/while
  200.0 18.4 %slice-start.1 = ((s8[12582912]{0:T(1024)(128)(4,1)}), s8[4194304]{0:T(1024)(128)(4,1)S(1)}, s32[]{:S(2)}) async-start(s8[12582912]{0:T(1024)(128)(4,1)} %bitcast.125), calls=%async_computation.4 | async-start | bytes 8388608 | tf_op jit(solution)/shard_map/while
  212.5 5.9 %slice-start.2 = ((s8[12582912]{0:T(1024)(128)(4,1)}), s8[4194304]{0:T(1024)(128)(4,1)S(1)}, s32[]{:S(2)}) async-start(s8[12582912]{0:T(1024)(128)(4,1)} %bitcast.125), calls=%async_computation.5 | async-start | bytes 8388608 | tf_op jit(solution)/shard_map/while
  226.6 4.5 copy-start
  231.5 7.0 %slice-start.3 = ((s8[6291456]{0:T(1024)(128)(4,1)}), s8[4194304]{0:T(1024)(128)(4,1)S(1)}, s32[]{:S(2)}) async-start(s8[6291456]{0:T(1024)(128)(4,1)} %bitcast.129), calls=%async_computation.6 | async-start | bytes 8388608 | tf_op jit(solution)/shard_map/while
  251.3 18.4 %slice-start = ((s8[12582912]{0:T(1024)(128)(4,1)}), s8[4194304]{0:T(1024)(128)(4,1)S(1)}, s32[]{:S(2)}) async-start(s8[12582912]{0:T(1024)(128)(4,1)} %bitcast.125), calls=%async_computation.3 | async-start | bytes 8388608 | tf_op jit(solution)/shard_map/while
  251.3 18.4 %slice-start.1 = ((s8[12582912]{0:T(1024)(128)(4,1)}), s8[4194304]{0:T(1024)(128)(4,1)S(1)}, s32[]{:S(2)}) async-start(s8[12582912]{0:T(1024)(128)(4,1)} %bitcast.125), calls=%async_computation.4 | async-start | bytes 8388608 | tf_op jit(solution)/shard_map/while
  263.8 5.9 %slice-start.2 = ((s8[12582912]{0:T(1024)(128)(4,1)}), s8[4194304]{0:T(1024)(128)(4,1)S(1)}, s32[]{:S(2)}) async-start(s8[12582912]{0:T(1024)(128)(4,1)} %bitcast.125), calls=%async_computation.5 | async-start | bytes 8388608 | tf_op jit(solution)/shard_map/while
  278.0 4.5 copy-start
  282.8 7.0 %slice-start.3 = ((s8[6291456]{0:T(1024)(128)(4,1)}), s8[4194304]{0:T(1024)(128)(4,1)S(1)}, s32[]{:S(2)}) async-start(s8[6291456]{0:T(1024)(128)(4,1)} %bitcast.129), calls=%async_computation.6 | async-start | bytes 8388608 | tf_op jit(solution)/shard_map/while
  302.7 18.4 %slice-start = ((s8[12582912]{0:T(1024)(128)(4,1)}), s8[4194304]{0:T(1024)(128)(4,1)S(1)}, s32[]{:S(2)}) async-start(s8[12582912]{0:T(1024)(128)(4,1)} %bitcast.125), calls=%async_computation.3 | async-start | bytes 8388608 | tf_op jit(solution)/shard_map/while
  302.7 18.4 %slice-start.1 = ((s8[12582912]{0:T(1024)(128)(4,1)}), s8[4194304]{0:T(1024)(128)(4,1)S(1)}, s32[]{:S(2)}) async-start(s8[12582912]{0:T(1024)(128)(4,1)} %bitcast.125), calls=%async_computation.4 | async-start | bytes 8388608 | tf_op jit(solution)/shard_map/while
  315.2 5.9 %slice-start.2 = ((s8[12582912]{0:T(1024)(128)(4,1)}), s8[4194304]{0:T(1024)(128)(4,1)S(1)}, s32[]{:S(2)}) async-start(s8[12582912]{0:T(1024)(128)(4,1)} %bitcast.125), calls=%async_computation.5 | async-start | bytes 8388608 | tf_op jit(solution)/shard_map/while
  329.3 4.5 copy-start
  (4 other events, 9.8 us)
Sparse Core Ops, SparseCore 0:
  9.8 48.9 all-gather.3
  60.7 44.6 all-gather.5
  350.2 157.3 all-reduce.5
where the time goes:
time: 521 us; the launch traced here: 520 us
  waiting for transfers between devices  205 us (39%)
  matrix products  137 us (26%)
  local copies, waits for them, and re-layouts  83.2 us (16%)
  blocking collectives  46.4 us (9%)
  other arithmetic  32.9 us (6%)
  between operations  14.5 us (3%)
    unnamed x4, waiting for transfers between devices  129 us
    while x64, local copies, waits for them, and re-layouts  63.1 us
    dot_general x4, matrix products, accumulate(): jnp.dot(spread, first_part.reshape(slot_total, CB * feature_count), preci...  48.1 us
    all_gather x1, waiting for transfers between devices, on_device(): lax.all_gather(means, 'dp', axis=0, tiled=True)  46.5 us
    dot_general x4, matrix products, accumulate(): jnp.dot(spread, second_part.reshape(slot_total, CB * feature_count), prec...  32.8 us
    all_gather x1, waiting for transfers between devices, on_device(): lax.all_gather(inv_var, 'dp', axis=0, tiled=True)  28.7 us
    unnamed x1, blocking collectives  26.5 us
    all_gather x1, blocking collectives, on_device(): lax.all_gather(log_weight, 'dp', axis=0, tiled=True)  20 us
  transfers between devices with their start and end apart: 3, of which 3 were waited for; matrix products, arithmetic and copies ran while one was open for 1% of the time, Pallas kernels for 0%

commit v1 on v0

--- a/solution.py
+++ b/solution.py
@@ -67,7 +67,9 @@
     held_blocks = means.shape[0] // CB
     all_means, all_inverse, all_logs = (
         lax.all_gather(means, "dp", axis=0, tiled=True),
-        lax.all_gather(inv_var, "dp", axis=0, tiled=True),
+        jnp.concatenate(
+            lax.all_to_all(jnp.stack([inv_var] * lax.axis_size("dp")), "dp", 0, 0), axis=0
+        ),
         lax.all_gather(log_weight, "dp", axis=0, tiled=True),
     )
     all_scaled = (all_inverse.astype(jnp.float32) * all_means.astype(jnp.float32)).astype(

time: 521 us -> 643 us (1.23)
  blocking collectives: 46.4 us -> 203 us
  waiting for transfers between devices: 205 us -> 132 us
  loops' own time: 0.92 us -> 18.2 us
  starting transfers between devices: 0.11 us -> 8.82 us
    all_gather x1, blocking collectives: 20 us -> 178 us  [on_device(): lax.all_gather(log_weight, 'dp', axis=0, tiled=True)]
    all_gather x1, waiting for transfers between devices: 46.5 us -> 0.02 us  [on_device(): lax.all_gather(means, 'dp', axis=0, tiled=True)]
    all_gather x1 -> x0, waiting for transfers between devices: 28.7 us -> none  [on_device(): lax.all_gather(inv_var, 'dp', axis=0, tiled=True)]
    another operation x1, loops' own time: 0.92 us -> 18.2 us  [on_device(): lax.scan(accumulate, initial, (row_groups, id_groups))]
    another operation x0 -> x2, local copies, waits for them, and re-layouts: none -> 11.6 us  [the longest x1 7.31 us: on_device(): inverse_flat = all_inverse.reshape(group_blocks, CB * feature_count)]
    convert_element_type x0 -> x1, other arithmetic: none -> 9.57 us  [on_device(): (all_inverse.astype(jnp.float32) * all_means.astype(jnp.float32)).astype(...]
    all_to_all x0 -> x1, starting transfers between devices: none -> 8.75 us  [on_device(): lax.all_to_all(jnp.stack([inv_var] * lax.axis_size('dp')), 'dp', 0, 0)]
    reshape x1 -> x0, local copies, waits for them, and re-layouts: 7.31 us -> none  [on_device(): inverse_flat = all_inverse.reshape(group_blocks, CB * feature_count)]
  transfers between devices with their start and end apart: 3 -> 3, of which waited for: 3 -> 1; matrix products, arithmetic and copies ran while one was open for 1% -> 1% of each run, Pallas kernels for 0% -> 0%
where the time goes in v1:
time: 643 us; the launch traced here: 637 us
  blocking collectives  203 us (32%)
  matrix products  137 us (21%)
  waiting for transfers between devices  132 us (21%)
  local copies, waits for them, and re-layouts  86.8 us (13%)
  other arithmetic  35.8 us (6%)
  loops' own time  18.2 us (3%)
  between operations  15.2 us (2%)
  starting transfers between devices  8.82 us (1%)
    all_gather x1, blocking collectives, on_device(): lax.all_gather(log_weight, 'dp', axis=0, tiled=True)  178 us
    unnamed x3, waiting for transfers between devices  132 us
    while x64, local copies, waits for them, and re-layouts  63.1 us
    dot_general x4, matrix products, accumulate(): jnp.dot(spread, first_part.reshape(slot_total, CB * feature_count), preci...  48.1 us
    dot_general x4, matrix products, accumulate(): jnp.dot(spread, second_part.reshape(slot_total, CB * feature_count), prec...  32.8 us
    unnamed x1, blocking collectives  24.9 us
    another operation x1, loops' own time, on_device(): lax.scan(accumulate, initial, (row_groups, id_groups))  18.2 us
    dot_general x4, matrix products, block_terms(): jnp.dot(pick_bf, scaled_flat, preferred_element_type=jnp.float32)  15.9 us
  transfers between devices with their start and end apart: 3, of which 1 were waited for; matrix products, arithmetic and copies ran while one was open for 1% of the time, Pallas kernels for 0%

profile of v1, /device:TPU:2, one launch (start us, length us, event | category | flops | bytes accessed | tf_op | source)
XLA Modules:
  0.0 637.1 jit_solution(17060317489978299087)
XLA Ops:
  11.5 8.7 %all-to-all-start = ((bf16[16,256,768]{2,1,0:T(8,128)(2,1)}), bf16[16,256,768]{2,1,0:T(8,128)(2,1)}, u32[]{:S(2)}, u32[]{:S(2)}) async-start(bf16[16,256,768]{2,1,0:T(8,128)(2,1)} %stack.2), calls=%async_computation | async-start | bytes 12582912 | tf_op jit(solution)/shard_map/all_to_all | solution.py:71
  21.1 178.1 %all-gather = bf16[16,1,256]{2,1,0:T(2,128)(2,1)S(1)} all-gather(bf16[1,1,256]{2,1,0:T(2,128)(2,1)S(1)} %reshape.132), channel_id=1, replica_groups=mesh['dp'=16,'comp'=16] {'dp'}, dimensions={0}, use_global_device_ids=true | all-gather | bytes 8704 | tf_op jit(solution)/shard_map/all_gather | solution.py:73
  199.3 4.6 log_reduce_fusion
  204.0 9.6 %fusion.32 = (bf16[4096,768]{1,0:T(8,128)(2,1)}, f32[4096]{0:T(1024)S(1)}) fusion(bf16[4096,768]{1,0:T(8,128)(2,1)} %all-gather.3.cloned.1.call-done, bf16[16,256,768]{2,1,0:T(8,128)(2,1)} %all-to-all-done), kind=kLoop, calls=%fused_computation.46 | loop fusion | flops 18870272 | bytes 18890752 | tf_op jit(solution)/shard_map/convert_element_type | solution.py:75
  213.6 7.3 %reshape.114 = bf16[32,98304]{1,0:T(8,128)(2,1)} reshape(bf16[4096,768]{1,0:T(8,128)(2,1)} %get-tuple-element.180) | data formatting | bytes 12582912 | tf_op jit(solution)/shard_map/reshape | solution.py:80
  220.9 7.3 %reshape_reshape.3 = bf16[32,98304]{1,0:T(8,128)(2,1)} reshape(bf16[16,256,768]{2,1,0:T(8,128)(2,1)} %all-to-all-done) | data formatting | bytes 12582912 | tf_op jit(solution)/shard_map/reshape;reshape | solution.py:81
  228.2 221.0 %while.18 = (s32[]{:T(128)}, f32[32,128]{1,0:T(8,128)S(1)}, f32[32,98304]{1,0:T(8,128)}, f32[32,98304]{1,0:T(8,128)}, f32[4,4,128]{2,1,0:T(4,128)S(1)}, /*index=...) while((s32[]{:T(128)}, f32[32,128]{1,0:T(8,128)S(1)}, ...), condition=%wide.region_6.7_spmd.clone.clone, body=%wide.region_2.6_spmd.clone.clone.sunk | while | flops 3042191872 | bytes 255429680 | solution.py:118
  259.1 6.3 copy.25
  265.4 10.7 %convolution_add_fusion.7 = f32[32,98304]{1,0:T(8,128)} fusion(f32[16,98304]{1,0:T(8,128)} %bitcast.128, f32[32,98304]{1,0:T(8,128)} %get-tuple-element.271, pred[]{:T(512)S(6)} %compare.6, s32[16]{0:T(128)S(1)} %eq.108), kind=kOutput, calls=%fused_computation.2.clone.1 | convolution fusion | flops 610271744 | bytes 31457344 | tf_op jit(solution)/shard_map/while/body/eval_jaxpr/dot_general | solution.py:100
  282.0 8.2 %convolution_add_fusion.8 = f32[32,98304]{1,0:T(8,128)S(1)} fusion(f32[16,98304]{1,0:T(8,128)S(1)} %bitcast.129, f32[32,98304]{1,0:T(8,128)S(1)} %bitcast.135, pred[]{:T(512)S(6)} %compare.6, s32[16]{0:T(128)S(1)} %eq.108), kind=kOutput, calls=%fused_computation.1.clone.1 | convolution fusion | flops 610271744 | bytes 31457344 | tf_op jit(solution)/shard_map/while/body/eval_jaxpr/dot_general | solution.py:105
  290.2 4.5 copy-done
  308.6 6.3 copy.25
  314.9 12.5 %convolution_add_fusion.7 = f32[32,98304]{1,0:T(8,128)} fusion(f32[16,98304]{1,0:T(8,128)} %bitcast.128, f32[32,98304]{1,0:T(8,128)} %get-tuple-element.271, pred[]{:T(512)S(6)} %compare.6, s32[16]{0:T(128)S(1)} %eq.108), kind=kOutput, calls=%fused_computation.2.clone.1 | convolution fusion | flops 610271744 | bytes 31457344 | tf_op jit(solution)/shard_map/while/body/eval_jaxpr/dot_general | solution.py:100
  333.4 8.2 %convolution_add_fusion.8 = f32[32,98304]{1,0:T(8,128)S(1)} fusion(f32[16,98304]{1,0:T(8,128)S(1)} %bitcast.129, f32[32,98304]{1,0:T(8,128)S(1)} %bitcast.135, pred[]{:T(512)S(6)} %compare.6, s32[16]{0:T(128)S(1)} %eq.108), kind=kOutput, calls=%fused_computation.1.clone.1 | convolution fusion | flops 610271744 | bytes 31457344 | tf_op jit(solution)/shard_map/while/body/eval_jaxpr/dot_general | solution.py:105
  360.0 6.3 copy.25
  366.3 12.5 %convolution_add_fusion.7 = f32[32,98304]{1,0:T(8,128)} fusion(f32[16,98304]{1,0:T(8,128)} %bitcast.128, f32[32,98304]{1,0:T(8,128)} %get-tuple-element.271, pred[]{:T(512)S(6)} %compare.6, s32[16]{0:T(128)S(1)} %eq.108), kind=kOutput, calls=%fused_computation.2.clone.1 | convolution fusion | flops 610271744 | bytes 31457344 | tf_op jit(solution)/shard_map/while/body/eval_jaxpr/dot_general | solution.py:100
  384.7 8.2 %convolution_add_fusion.8 = f32[32,98304]{1,0:T(8,128)S(1)} fusion(f32[16,98304]{1,0:T(8,128)S(1)} %bitcast.129, f32[32,98304]{1,0:T(8,128)S(1)} %bitcast.135, pred[]{:T(512)S(6)} %compare.6, s32[16]{0:T(128)S(1)} %eq.108), kind=kOutput, calls=%fused_computation.1.clone.1 | convolution fusion | flops 610271744 | bytes 31457344 | tf_op jit(solution)/shard_map/while/body/eval_jaxpr/dot_general | solution.py:105
  411.4 6.3 copy.25
  417.6 12.5 %convolution_add_fusion.7 = f32[32,98304]{1,0:T(8,128)} fusion(f32[16,98304]{1,0:T(8,128)} %bitcast.128, f32[32,98304]{1,0:T(8,128)} %get-tuple-element.271, pred[]{:T(512)S(6)} %compare.6, s32[16]{0:T(128)S(1)} %eq.108), kind=kOutput, calls=%fused_computation.2.clone.1 | convolution fusion | flops 610271744 | bytes 31457344 | tf_op jit(solution)/shard_map/while/body/eval_jaxpr/dot_general | solution.py:100
  436.1 8.2 %convolution_add_fusion.8 = f32[32,98304]{1,0:T(8,128)S(1)} fusion(f32[16,98304]{1,0:T(8,128)S(1)} %bitcast.129, f32[32,98304]{1,0:T(8,128)S(1)} %bitcast.135, pred[]{:T(512)S(6)} %compare.6, s32[16]{0:T(128)S(1)} %eq.108), kind=kOutput, calls=%fused_computation.1.clone.1 | convolution fusion | flops 610271744 | bytes 31457344 | tf_op jit(solution)/shard_map/while/body/eval_jaxpr/dot_general | solution.py:105
  449.2 7.9 %convert_element_type.64 = bf16[32,98304]{1,0:T(8,128)(2,1)} convert(f32[32,98304]{1,0:T(8,128)} %get-tuple-element.68) | non-fusion elementwise | flops 3145728 | bytes 18874368 | tf_op jit(solution)/shard_map/convert_element_type | solution.py:124
  457.1 7.8 %convert_element_type.65 = bf16[32,98304]{1,0:T(8,128)(2,1)} convert(f32[32,98304]{1,0:T(8,128)} %get-tuple-element.69) | non-fusion elementwise | flops 3145728 | bytes 18874368 | tf_op jit(solution)/shard_map/convert_element_type | solution.py:127
  466.9 24.9 %all-reduce = bf16[32,128]{1,0:T(8,128)(2,1)S(1)} all-reduce(bf16[32,128]{1,0:T(8,128)(2,1)S(1)} %convert_element_type.63), channel_id=2, replica_groups=mesh['dp'=16,'comp'=16] {'dp'}, use_global_device_ids=true, to_apply=%region_7.8.clone | all-reduce | flops 4096 | bytes 16384
  493.0 131.2 %all-reduce.6.cloned.1.call-done = (bf16[32,98304]{1,0:T(8,128)(2,1)}, bf16[32,98304]{1,0:T(8,128)(2,1)}) async-done(((bf16[32,98304]{1,0:T(8,128)(2,1)}, bf16[32,98304]{1,0:T(8,128)(2,1)}), (bf16[32,98304]{1,0:T(8,128)(2,1)}, bf16[32,98304]{1,0:T(8,128)(2,1)})) %all-reduce.6.cloned.1.call-update) | async-done | bytes 12582928
  (154 shorter events, 105.7 us)
Async XLA Ops:
  11.5 9.6 %copy-start.2 = (bf16[256]{0:T(256)(128)(2,1)S(1)}, bf16[256]{0:T(256)(128)(2,1)}, u32[]{:S(2)}) copy-start(bf16[256]{0:T(256)(128)(2,1)} %param.11) | copy-start | bytes 1540
  11.5 187.7 %copy-start.1 = (s32[16,4]{0,1:T(4,128)S(1)}, s32[16,4]{0,1:T(4,128)}, u32[]{:S(2)}) copy-start(s32[16,4]{0,1:T(4,128)} %param.8) | copy-start | bytes 772
  11.5 187.8 %all-to-all-start = ((bf16[16,256,768]{2,1,0:T(8,128)(2,1)}), bf16[16,256,768]{2,1,0:T(8,128)(2,1)}, u32[]{:S(2)}, u32[]{:S(2)}) async-start(bf16[16,256,768]{2,1,0:T(8,128)(2,1)} %stack.2), calls=%async_computation | async-start | bytes 12582912 | tf_op jit(solution)/shard_map/all_to_all | solution.py:71
  20.3 183.8 %all-gather.3.cloned.1.call-start = ((), (), s32[]{:S(2)}) async-start(), calls=%async_computation.1 | async-start | bytes 6684672 | tf_op jit(solution)/shard_map/all_gather | solution.py:69
  21.0 603.2 %all-reduce.6.cloned.1.call-start = ((), (), s32[]{:S(2)}) async-start(), calls=%async_computation.2 | async-start | bytes 25165824
  245.6 7.0 %slice-start.3 = ((s8[6291456]{0:T(1024)(128)(4,1)}), s8[4194304]{0:T(1024)(128)(4,1)S(1)}, s32[]{:S(2)}) async-start(s8[6291456]{0:T(1024)(128)(4,1)} %bitcast.138), calls=%async_computation.6 | async-start | bytes 8388608 | tf_op jit(solution)/shard_map/while
  265.4 16.6 %slice-start = ((s8[12582912]{0:T(1024)(128)(4,1)}), s8[4194304]{0:T(1024)(128)(4,1)S(1)}, s32[]{:S(2)}) async-start(s8[12582912]{0:T(1024)(128)(4,1)} %bitcast.134), calls=%async_computation.3 | async-start | bytes 8388608 | tf_op jit(solution)/shard_map/while
  265.4 16.6 %slice-start.1 = ((s8[12582912]{0:T(1024)(128)(4,1)}), s8[4194304]{0:T(1024)(128)(4,1)S(1)}, s32[]{:S(2)}) async-start(s8[12582912]{0:T(1024)(128)(4,1)} %bitcast.134), calls=%async_computation.4 | async-start | bytes 8388608 | tf_op jit(solution)/shard_map/while
  276.1 5.9 slice-start.2
  290.2 4.5 copy-start
  295.1 7.0 %slice-start.3 = ((s8[6291456]{0:T(1024)(128)(4,1)}), s8[4194304]{0:T(1024)(128)(4,1)S(1)}, s32[]{:S(2)}) async-start(s8[6291456]{0:T(1024)(128)(4,1)} %bitcast.138), calls=%async_computation.6 | async-start | bytes 8388608 | tf_op jit(solution)/shard_map/while
  314.9 18.4 %slice-start = ((s8[12582912]{0:T(1024)(128)(4,1)}), s8[4194304]{0:T(1024)(128)(4,1)S(1)}, s32[]{:S(2)}) async-start(s8[12582912]{0:T(1024)(128)(4,1)} %bitcast.134), calls=%async_computation.3 | async-start | bytes 8388608 | tf_op jit(solution)/shard_map/while
  314.9 18.4 %slice-start.1 = ((s8[12582912]{0:T(1024)(128)(4,1)}), s8[4194304]{0:T(1024)(128)(4,1)S(1)}, s32[]{:S(2)}) async-start(s8[12582912]{0:T(1024)(128)(4,1)} %bitcast.134), calls=%async_computation.4 | async-start | bytes 8388608 | tf_op jit(solution)/shard_map/while
  327.4 5.9 slice-start.2
  341.6 4.5 copy-start
  346.4 7.0 %slice-start.3 = ((s8[6291456]{0:T(1024)(128)(4,1)}), s8[4194304]{0:T(1024)(128)(4,1)S(1)}, s32[]{:S(2)}) async-start(s8[6291456]{0:T(1024)(128)(4,1)} %bitcast.138), calls=%async_computation.6 | async-start | bytes 8388608 | tf_op jit(solution)/shard_map/while
  366.3 18.4 %slice-start = ((s8[12582912]{0:T(1024)(128)(4,1)}), s8[4194304]{0:T(1024)(128)(4,1)S(1)}, s32[]{:S(2)}) async-start(s8[12582912]{0:T(1024)(128)(4,1)} %bitcast.134), calls=%async_computation.3 | async-start | bytes 8388608 | tf_op jit(solution)/shard_map/while
  366.3 18.4 %slice-start.1 = ((s8[12582912]{0:T(1024)(128)(4,1)}), s8[4194304]{0:T(1024)(128)(4,1)S(1)}, s32[]{:S(2)}) async-start(s8[12582912]{0:T(1024)(128)(4,1)} %bitcast.134), calls=%async_computation.4 | async-start | bytes 8388608 | tf_op jit(solution)/shard_map/while
  378.8 5.9 slice-start.2
  392.9 4.5 copy-start
  397.8 7.0 %slice-start.3 = ((s8[6291456]{0:T(1024)(128)(4,1)}), s8[4194304]{0:T(1024)(128)(4,1)S(1)}, s32[]{:S(2)}) async-start(s8[6291456]{0:T(1024)(128)(4,1)} %bitcast.138), calls=%async_computation.6 | async-start | bytes 8388608 | tf_op jit(solution)/shard_map/while
  417.6 18.4 %slice-start = ((s8[12582912]{0:T(1024)(128)(4,1)}), s8[4194304]{0:T(1024)(128)(4,1)S(1)}, s32[]{:S(2)}) async-start(s8[12582912]{0:T(1024)(128)(4,1)} %bitcast.134), calls=%async_computation.3 | async-start | bytes 8388608 | tf_op jit(solution)/shard_map/while
  417.6 18.4 %slice-start.1 = ((s8[12582912]{0:T(1024)(128)(4,1)}), s8[4194304]{0:T(1024)(128)(4,1)S(1)}, s32[]{:S(2)}) async-start(s8[12582912]{0:T(1024)(128)(4,1)} %bitcast.134), calls=%async_computation.4 | async-start | bytes 8388608 | tf_op jit(solution)/shard_map/while
  430.1 5.9 slice-start.2
  (6 other events, 17.4 us)
Sparse Core Ops, SparseCore 0:
  22.9 133.8 all-gather.2
  465.1 159.0 all-reduce.5
